TPU v7x, 32 devices: a whole 2x2x4 slice. The times are simulated.
32 devices in a mesh: samples: 8 (over z, y), params: 4 (over x, core).
Axes of the slice: x: 2, y: 2, z: 4, core: 2. Of those that a mesh axis runs over, the one named last changes fastest.
Arguments:
- occupations: int32 [512, 152], P('samples'), may hold values from 0 to 1, as said below
- connection_counts: int32 [512], P('samples'), may hold values from 0 to 3072, as said below
- connection_orbitals: int32 [4, 24576], P(None, ('samples', 'params')), may hold values from 0 to 151, as said below
- connection_elements: float32 [2, 24576], P(None, ('samples', 'params')), may hold values from -2 to 2
- laser_step: int32 [], replicated, may hold values from 0 to 3999
- first_weight: bfloat16 [152, 1024], replicated, may hold values from -4 to 4
- first_bias: float32 [1024], replicated, may hold values from -3 to 3
- second_weight: bfloat16 [1024, 256], P('params'), may hold values from -1.25 to 1.25
- readout: float32 [2, 256], replicated, may hold values from -0.375 to 0.375
Outputs:
- local_energy: float32 [2, 512], P(None, 'samples')
- change: float32 [2, 512], P(None, 'samples')
Inputs may be any that keep to these rules, and one draw needn't show every extreme that they name: `occupations`: each row has exactly 76 ones. `connection_counts`: the connections of block b of 64 consecutive samples fill the first slots q of that block in order of sample; the counts of a block sum to at most 3072, and to exactly 3072 in some block. `connection_orbitals`: the 4 orbitals of a slot are distinct; unused slots hold arbitrary orbitals in the range.
All inputs are finite; a program needn't handle non-finite values.
Results may differ from a plain program's by a relative error of at most 0.0099.
Values may be sent and summed in bfloat16 or wider, within the bound.
No kernel may reach another device: no remote copies, remote signals or barrier semaphores. Data moves between devices by JAX's collectives and lax.ppermute only.
A program may use at most 64 MiB of HBM per device.

v0:
```python
import functools

import jax
import jax.numpy as jnp
from jax import lax
from jax.experimental import pallas as pl
from jax.experimental.pallas import tpu as pltpu
from jax.sharding import Mesh, PartitionSpec as P

ITERS = 2


FIELD_SCALE = 0.8
FIELD_RATE = 0.0123
DIAG_SHIFT = 0.01
F32 = jnp.float32
BF16 = jnp.bfloat16
ROWS = 256
COLLECT_WEIGHT = 1e10
VMEM_LIMIT = 48 * 1024 * 1024


def dot(a, b, dims):
    return lax.dot_general(a, b, (dims, ((), ())), preferred_element_type=F32)


def split(x):
    high = lax.reduce_precision(x, 8, 7)
    return high.astype(BF16), (x - high).astype(BF16)


def parts(x):
    high = x.astype(BF16)
    rest = x - high.astype(F32)
    middle = rest.astype(BF16)
    return high, middle, (rest - middle.astype(F32)).astype(BF16)


def iota(shape, dim):
    return lax.broadcasted_iota(jnp.int32, shape, dim)


def call(kernel, count, out_shape, scratch=(), name=None, copies=False, flops=0, transcendentals=0):
    vmem = pl.BlockSpec(memory_space=pltpu.VMEM)
    far = pl.BlockSpec(memory_space=pltpu.HBM)
    return pl.pallas_call(
        kernel,
        out_shape=out_shape,
        in_specs=[far if copies else vmem] * count,
        out_specs=jax.tree.map(lambda _: vmem, out_shape),
        scratch_shapes=scratch,
        compiler_params=pltpu.CompilerParams(vmem_limit_bytes=VMEM_LIMIT),
        cost_estimate=pl.CostEstimate(
            flops=int(flops),
            transcendentals=int(transcendentals),
            bytes_accessed=sum(x.size * x.dtype.itemsize for x in jax.tree.leaves(out_shape)),
        ),
        name=name,
    )


def slot_hidden_kernel(
    spread,
    counts_hbm,
    orbitals_hbm,
    occ_hbm,
    w1_hbm,
    bias_hbm,
    elements_hbm,
    readout_hbm,
    own_hbm,
    hidden_ref,
    owner_ref,
    elements_ref,
    w1_ref,
    bias_ref,
    readout_ref,
    own_ref,
    occupied_ref,
    counts_ref,
    orbitals_ref,
    occ_ref,
    sems,
):
    here, orbitals = occ_ref.shape
    updates, slots = orbitals_ref.shape
    pairs = (
        (counts_hbm, counts_ref),
        (occ_hbm, occ_ref),
        (w1_hbm, w1_ref),
        (bias_hbm, bias_ref),
        (orbitals_hbm, orbitals_ref),
        (elements_hbm, elements_ref),
        (readout_hbm, readout_ref),
        (own_hbm, own_ref),
    )
    copies = [pltpu.make_async_copy(a, b, sems.at[i]) for i, (a, b) in enumerate(pairs)]
    for copy in copies:
        copy.start()
    chip, core = lax.axis_index("chip"), lax.axis_index("core")
    place = chip * 2 + core
    copies[0].wait()
    counts = counts_ref[...].astype(F32)
    row, col = iota((here, here), 0), iota((here, here), 1)
    ends = jnp.sum(jnp.where(col <= row, counts, 0.0), axis=1, keepdims=True)
    starts = jnp.sum(jnp.where(col < row, counts, 0.0), axis=1, keepdims=True)
    positions = (place + spread * iota((1, slots), 1)).astype(F32)
    owner = jnp.where((starts <= positions) & (positions < ends), 1.0, 0.0).astype(BF16)
    owner_ref[...] = owner
    copies[1].wait()
    occupied = occ_ref[...].astype(F32).astype(BF16)
    occupied_ref[...] = occupied
    copies[2].wait()
    copies[3].wait()
    w1 = w1_ref[...]
    bias = bias_ref[...]
    hidden_ref[slots:, :] = jnp.tanh(dot(occupied, w1, ((1,), (0,))) + bias).astype(BF16)
    copies[4].wait()
    for start in range(0, slots, ROWS):
        stop = min(start + ROWS, slots)
        parent_occ = dot(occupied, owner[:, start:stop], ((0,), (0,)))
        columns = iota((orbitals, stop - start), 0)
        flipped = columns == orbitals_ref[0:1, start:stop]
        for u in range(1, updates):
            flipped = flipped | (columns == orbitals_ref[u : u + 1, start:stop])
        slot_occ = jnp.where(flipped, 1.0 - parent_occ, parent_occ).astype(BF16)
        pre = dot(slot_occ, w1, ((0,), (0,))) + bias
        hidden_ref[start:stop, :] = jnp.tanh(pre).astype(BF16)
    copies[5].wait()
    copies[6].wait()
    copies[7].wait()


def slot_energy_kernel(
    shifts, field_ref, hidden_ref, owner_ref, elements_ref, readout_ref, *refs
):
    shard_refs, (send_ref, second_ref) = refs[: len(shifts)], refs[len(shifts) :]
    here, slots = owner_ref.shape
    chips = lax.axis_size("chip")
    chip, core = lax.axis_index("chip"), lax.axis_index("core")
    for (step, other), shard in zip(shifts, shard_refs):
        rows = shard.shape[0]
        source = lax.rem(chip + chips - step, chips) * 2 + (core ^ other)
        second_ref[pl.ds(pl.multiple_of(source * rows, rows), rows), :] = shard[...]
    mid = jnp.tanh(dot(second_ref[...], hidden_ref[...], ((0,), (1,))))
    readout = readout_ref[...].T
    logs_re = jnp.sum(mid * readout[:, 0:1], axis=0, keepdims=True)
    logs_im = jnp.sum(mid * readout[:, 1:2], axis=0, keepdims=True)
    owner = owner_ref[...]
    own = jnp.concatenate(parts(logs_re[:, slots:]) + parts(logs_im[:, slots:]), axis=0)
    parent = dot(own, owner, ((1,), (0,)))
    diff_re = logs_re[:, :slots] - (parent[0:1] + parent[1:2] + parent[2:3])
    diff_im = logs_im[:, :slots] - (parent[3:4] + parent[4:5] + parent[5:6])
    used = jnp.sum(owner.astype(F32), axis=0, keepdims=True) > 0.0
    weight = elements_ref[0:1, :] + field_ref[...] * elements_ref[1:2, :]
    scale = weight * jnp.exp(diff_re)
    contrib_re = jnp.where(used, scale * jnp.cos(diff_im), 0.0)
    contrib_im = jnp.where(used, scale * jnp.sin(diff_im), 0.0)
    contrib = jnp.concatenate(parts(contrib_re) + parts(contrib_im), axis=0)
    sums = dot(contrib, owner, ((1,), (1,)))
    partial_re = sums[0:1] + sums[1:2] + sums[2:3]
    partial_im = sums[3:4] + sums[4:5] + sums[5:6]
    row = jnp.concatenate([partial_re, partial_im], axis=1)
    send_ref[...] = jnp.broadcast_to(row[None], send_ref.shape)


def collect_kernel(entries, chips, received_ref, energy_ref):
    here = received_ref.shape[2] // 2
    block = lax.axis_index("samples")
    out_re, out_im = [], []
    peers = received_ref.shape[0]
    for entry in entries:
        first = lax.rem((block ^ entry) * chips + peers // 2, peers)
        row = received_ref[first]
        for k in range(1, chips):
            row = row + received_ref[first + k]
        out_re.append(row[:, :here])
        out_im.append(row[:, here:])
    energy_ref[...] = jnp.concatenate(
        [jnp.concatenate(out_re, axis=1), jnp.concatenate(out_im, axis=1)], axis=0
    )


def sample_values(packed_ref, w1_ref, bias_ref, second_ref, readout_ref, size):
    hidden = jnp.tanh(sample_pre(packed_ref, w1_ref, bias_ref, size)).astype(BF16)
    mid = jnp.tanh(dot(second_ref[...], hidden, ((0,), (1,))))
    slope = 1.0 - mid * mid
    readout = readout_ref[...].T
    return hidden, slope * readout[:, 0:1], slope * readout[:, 1:2]


def pack_kernel(mine_ref, moved_ref, after_ref, packed_ref):
    del after_ref
    blocks, here, orbitals = mine_ref.shape
    full = packed_ref.shape[1]
    pieces = [mine_ref[k] for k in range(blocks)] + [moved_ref[k] for k in range(blocks)]
    rest = orbitals - full
    for k, piece in enumerate(pieces):
        packed_ref[k * here : (k + 1) * here, :] = piece[:, :full]
    rests = [piece[:, full:].astype(F32) for piece in pieces]
    rests.append(jnp.zeros((here, full - rest * len(pieces)), F32))
    packed_ref[len(pieces) * here :, :] = jnp.concatenate(rests, axis=1).astype(BF16)


def sample_pre(packed_ref, w1_ref, bias_ref, size):
    full = packed_ref.shape[1]
    here = packed_ref.shape[0] - size
    rest = w1_ref.shape[0] - full
    tail = packed_ref[size:, :].astype(F32)
    rests = [tail[:, k * rest : (k + 1) * rest] for k in range(size // here)]
    tail = jnp.concatenate(rests, axis=0).astype(BF16)
    pre = dot(packed_ref[:size, :], w1_ref[:full, :], ((1,), (0,)))
    return pre + dot(tail, w1_ref[full:, :], ((1,), (0,))) + bias_ref[...]


def near_half_kernel(packed_ref, w1_ref, bias_ref, second_ref, readout_ref, hidden_ref, overlap_ref, re_ref, im_ref):
    size = hidden_ref.shape[0]
    hidden, re_ref[...], im_ref[...] = sample_values(packed_ref, w1_ref, bias_ref, second_ref, readout_ref, size)
    hidden_ref[...] = hidden
    overlap_ref[...] = dot(hidden, hidden, ((1,), (1,)))


def far_half_kernel(
    packed_ref,
    w1_ref,
    bias_ref,
    second_ref,
    readout_ref,
    hidden_ref,
    overlap_ref,
    near_re_ref,
    near_im_ref,
    overlap_out_ref,
    re_ref,
    im_ref,
):
    size = hidden_ref.shape[0]
    total = 2 * size
    hidden, re, im = sample_values(packed_ref, w1_ref, bias_ref, second_ref, readout_ref, size)
    re_ref[:, :size] = near_re_ref[...]
    im_ref[:, :size] = near_im_ref[...]
    re_ref[:, size:] = re
    im_ref[:, size:] = im
    near = hidden_ref[...]

    def put(row, col, overlap):
        high = overlap.astype(BF16)
        columns = slice(col * size, (col + 1) * size)
        overlap_out_ref[row * size : (row + 1) * size, columns] = high
        low = (overlap - high.astype(F32)).astype(BF16)
        overlap_out_ref[total + row * size : total + (row + 1) * size, columns] = low
        overlap_out_ref[2 * total + row * size : 2 * total + (row + 1) * size, columns] = high

    put(0, 0, overlap_ref[...])
    put(0, 1, dot(near, hidden, ((1,), (1,))))
    put(1, 0, dot(hidden, near, ((1,), (1,))))
    put(1, 1, dot(hidden, hidden, ((1,), (1,))))


def solve(energy, gram):
    total = energy.shape[1]
    centered = energy - jnp.mean(energy, axis=1, keepdims=True)
    res_c = jnp.concatenate([centered[1:2], -centered[0:1]], axis=0) / total
    res_y = gram(res_c)
    dir_c, dir_y = res_c, res_y
    norm_now = full_sum(res_c * res_y)
    cross, square = norm_now, full_sum(res_y * res_y)
    change = jnp.zeros_like(res_y)
    for turn in range(ITERS):
        alpha = norm_now / (square / total + DIAG_SHIFT * cross)
        change = change + alpha * dir_y
        if turn + 1 < ITERS:
            img_c = dir_y / total + DIAG_SHIFT * dir_c
            img_y = gram(dir_y) / total + DIAG_SHIFT * dir_y
            res_c = res_c - alpha * img_c
            res_y = res_y - alpha * img_y
            norm_next = full_sum(res_c * res_y)
            mixed = full_sum(res_c * dir_y) + full_sum(dir_c * res_y)
            squares = full_sum(res_y * res_y), full_sum(res_y * dir_y)
            beta = norm_next / norm_now
            cross = norm_next + beta * mixed + beta * beta * cross
            square = squares[0] + 2.0 * beta * squares[1] + beta * beta * square
            dir_c = res_c + beta * dir_c
            dir_y = res_y + beta * dir_y
            norm_now = norm_next
    return change


def full_sum(x):
    return jnp.sum(jnp.sum(x, axis=1, keepdims=True), axis=0, keepdims=True)


def project(lifted, slope_re, slope_im):
    raw = jnp.concatenate(
        [jnp.sum(lifted * slope_re, axis=0, keepdims=True), jnp.sum(lifted * slope_im, axis=0, keepdims=True)],
        axis=0,
    )
    return raw - jnp.mean(raw, axis=1, keepdims=True)


def solve_kernel(mine_ref, other_ref, overlap_ref, re_ref, im_ref, local_ref, change_ref):
    width = local_ref.shape[1]
    energy = mine_ref[...] + other_ref[...]
    local_ref[...] = energy[:, :width]

    def gram(c):
        back = re_ref[...] * c[0:1] + im_ref[...] * c[1:2]
        high = back.astype(BF16)
        low = (back - high.astype(F32)).astype(BF16)
        lifted = dot(jnp.concatenate([high, high, low], axis=1), overlap_ref[...], ((1,), (0,)))
        return project(lifted, re_ref[...], im_ref[...])

    change_ref[...] = solve(energy, gram)[:, :width]


def wide_solve(energy, occ_stack, first_weight, bias_row, second, readout):
    here = occ_stack.shape[1]
    occupied = occ_stack.reshape(-1, occ_stack.shape[2])
    pre = dot(occupied, first_weight, ((1,), (0,))) + bias_row
    hidden = jnp.tanh(pre).astype(BF16)
    mid = jnp.tanh(dot(second, hidden, ((0,), (1,))))
    slope = 1.0 - mid * mid
    slope_re = slope * readout[0][:, None]
    slope_im = slope * readout[1][:, None]

    def gram(c):
        high, low = split(slope_re * c[0:1] + slope_im * c[1:2])
        high, low = split(dot(high, hidden, ((1,), (0,))) + dot(low, hidden, ((1,), (0,))))
        lifted = dot(high, hidden, ((1,), (1,))) + dot(low, hidden, ((1,), (1,)))
        return project(lifted, slope_re, slope_im)

    return energy[:, :here], solve(energy, gram)[:, :here]


def swap(x, axis, bit):
    return lax.ppermute(x, axis, [(i, i ^ bit) for i in range(lax.axis_size(axis))])


def shift(x, axis, step):
    size = lax.axis_size(axis)
    return lax.ppermute(x, axis, [(i, (i + step) % size) for i in range(size)])


def exchange_all(send):
    peers = send.shape[0]
    return lax.all_to_all(
        send,
        ("samples", "chip"),
        0,
        0,
        axis_index_groups=[[(k + peers // 2) % peers for k in range(peers)]],
        tiled=True,
    )


def powers(size):
    return [1 << k for k in reversed(range((size - 1).bit_length()))]


def body(
    occupations,
    connection_counts,
    connection_orbitals,
    connection_elements,
    laser_step,
    first_weight,
    first_bias,
    second_weight,
    readout,
):
    here, orbitals = occupations.shape
    slots = connection_orbitals.shape[1]
    wide, narrow = first_weight.shape[1], second_weight.shape[1]
    chips = lax.axis_size("chip")
    spread = chips * lax.axis_size("core")
    blocks = lax.axis_size("samples")
    total = here * blocks
    bias_row = first_bias[None, :]
    field = FIELD_SCALE * jnp.sin(FIELD_RATE * laser_step.astype(F32)[None, None])

    bits = powers(blocks)
    bits = bits[-1:] + bits[:-1]
    entries = [0]
    for bit in bits:
        entries = entries + [e ^ bit for e in entries]
    moved = swap(occupations.astype(BF16)[None], "samples", bits[0])

    shifts, shards = [], []
    for step in range(1, chips):
        shifts.append((step, 0))
        shards.append(shift(second_weight, "chip", step))
    shifts.append((0, 1))
    shards.append(shift(second_weight, "core", 1))

    hidden, owner, elements, w1, bias, readout_near, own_shard, occupied = call(
        functools.partial(slot_hidden_kernel, spread),
        8,
        (
            jax.ShapeDtypeStruct((slots + here, wide), BF16),
            jax.ShapeDtypeStruct((here, slots), BF16),
            jax.ShapeDtypeStruct(connection_elements.shape, F32),
            jax.ShapeDtypeStruct(first_weight.shape, BF16),
            jax.ShapeDtypeStruct(bias_row.shape, F32),
            jax.ShapeDtypeStruct(readout.shape, F32),
            jax.ShapeDtypeStruct(second_weight.shape, BF16),
            jax.ShapeDtypeStruct(occupations.shape, BF16),
        ),
        [
            pltpu.VMEM((1, here), jnp.int32),
            pltpu.VMEM(connection_orbitals.shape, jnp.int32),
            pltpu.VMEM(occupations.shape, jnp.int32),
            pltpu.SemaphoreType.DMA((8,)),
        ],
        name="slot_hidden",
        copies=True,
        flops=2 * (slots + here) * orbitals * wide,
        transcendentals=(slots + here) * wide,
    )(
        *(
            pltpu.with_memory_space_constraint(x, pltpu.HBM)
            for x in (
                connection_counts[None, :],
                connection_orbitals,
                occupations,
                first_weight,
                bias_row,
                connection_elements,
                readout,
                second_weight,
            )
        ),
    )
    relayed, occupied, field = lax.optimization_barrier((shards[: chips - 1], occupied, field))
    for step in range(1, chips):
        shifts.append((step, 1))
        shards.append(shift(relayed[step - 1], "core", 1))
    shifts.append((0, 0))
    stack = jnp.concatenate([occupied[None], moved], axis=0)
    moved = swap(stack, "samples", bits[1])

    send, second = call(
        functools.partial(slot_energy_kernel, tuple(shifts)),
        5 + len(shifts),
        (
            jax.ShapeDtypeStruct((blocks * chips, 1, 2 * here), F32),
            jax.ShapeDtypeStruct((wide, narrow), BF16),
        ),
        name="slot_energy",
        flops=2 * (slots + here) * wide * narrow,
        transcendentals=(slots + here) * narrow,
    )(field, hidden, owner, elements, readout_near, *shards, own_shard)
    received = exchange_all(send)
    mine = call(
        functools.partial(collect_kernel, entries, chips),
        1,
        jax.ShapeDtypeStruct((2, total), F32),
        name="collect",
        flops=COLLECT_WEIGHT,
    )(received)
    other = swap(mine, "core", 1)

    for bit in bits[2:-1]:
        stack = jnp.concatenate([stack, moved], axis=0)
        moved = swap(stack, "samples", bit)
    if total > wide:
        stack = jnp.concatenate([stack, moved], axis=0)
        stack = jnp.concatenate([stack, swap(stack, "samples", bits[-1])], axis=0)
        return wide_solve(mine + other, stack, first_weight, bias_row, second, readout)

    half = total // 2
    weights = (w1, bias, second, readout_near)
    full = orbitals // 128 * 128
    packed = call(
        pack_kernel,
        3,
        jax.ShapeDtypeStruct((half + here, full), BF16),
        name="pack",
    )(stack, moved, second)
    far_packed = swap(packed, "samples", bits[-1])
    near = call(
        near_half_kernel,
        5,
        (
            jax.ShapeDtypeStruct((half, wide), BF16),
            jax.ShapeDtypeStruct((half, half), F32),
            jax.ShapeDtypeStruct((narrow, half), F32),
            jax.ShapeDtypeStruct((narrow, half), F32),
        ),
        name="near_half",
        flops=2 * half * wide * (orbitals + narrow + half),
        transcendentals=half * (wide + narrow),
    )(packed, *weights)
    overlap = call(
        far_half_kernel,
        9,
        (jax.ShapeDtypeStruct((3 * total, total), BF16),) + (jax.ShapeDtypeStruct((narrow, total), F32),) * 2,
        name="far_half",
        flops=2 * half * wide * (orbitals + narrow + 3 * half),
        transcendentals=half * (wide + narrow),
    )(far_packed, *weights, *near)
    return call(
        solve_kernel,
        5,
        (jax.ShapeDtypeStruct((2, here), F32),) * 2,
        name="solve",
        flops=ITERS * 6 * total * total * narrow,
    )(mine, other, *overlap)


def solution(mesh):
    blocks, spread = mesh.shape["samples"], mesh.shape["params"]
    fine = Mesh(mesh.devices.reshape(blocks, spread // 2, 2), ("samples", "chip", "core"))
    return jax.shard_map(
        body,
        mesh=fine,
        in_specs=(
            P("samples", None),
            P("samples"),
            P(None, ("samples", "chip", "core")),
            P(None, ("samples", "chip", "core")),
            P(),
            P(),
            P(),
            P(("chip", "core"), None),
            P(),
        ),
        out_specs=(P(None, "samples"), P(None, "samples")),
        check_vma=False,
    )
```

profile of v0, /device:TPU:0, one launch (start us, length us, event | category | flops | bytes accessed | tf_op | source)
XLA Modules:
  0.0 27.2 jit_solution(13390409920825209593)
XLA Ops:
  0.6 3.0 %collective-permute-start = (bf16[256,256]{1,0:T(8,128)(2,1)}, bf16[256,256]{1,0:T(8,128)(2,1)S(1)}, u32[]{:S(2)}, u32[]{:S(2)}) collective-permute-start(bf16[256,256]{1,0:T(8,128)(2,1)} %own_hbm.1), channel_id=1, source_target_pairs={{0,2},{2,0},{1,3},{3,1},{4,6},{6,4},{5,7},{7,5},{8,10},{10,8},{9,1... | collective-permute-start | bytes 393224 | tf_op jit(solution)/shard_map/ppermute | solution.py:341
  3.6 0.0 collective-permute-start.1
  3.6 0.8 %convert_bitcast_fusion = bf16[1,64,152]{2,1,0:T(8,128)(2,1)S(1)} fusion(s32[64,152]{1,0:T(8,128)} %occ_hbm.1), kind=kLoop, calls=%fused_computation.1 | loop fusion | flops 9728 | bytes 58368 | tf_op jit(solution)/shard_map/broadcast_in_dim | solution.py:386
  4.5 1.5 %collective-permute-start.4 = (bf16[1,64,152]{2,1,0:T(8,128)(2,1)S(1)}, bf16[1,64,152]{2,1,0:T(8,128)(2,1)S(1)}, u32[]{:S(2)}, u32[]{:S(2)}) collective-permute-start(bf16[1,64,152]{2,1,0:T(8,128)(2,1)S(1)} %convert_bitcast_fusion), channel_id=1, source_target_pairs={{0,4},{4,0},{8,12},{12,8},{16,20},{20,16},{24,28},{28,24},{1,5},{5... | collective-permute-start | bytes 58376 | tf_op jit(solution)/shard_map/ppermute | solution.py:336
  6.0 2.6 %slot_hidden.1 = (bf16[832,1024]{1,0:T(8,128)(2,1)S(1)}, bf16[64,768]{1,0:T(8,128)(2,1)S(1)}, f32[2,768]{1,0:T(2,128)S(1)}, bf16[152,1024]{1,0:T(8,128)(2,1)S(1)...) custom-call(s32[1,64]{1,0:T(1,128)} %bitcast.8, ...), custom_call_target="tpu_custom_call" | custom-call | flops 258998272 | bytes 2276352 | tf_op jit(solution)/shard_map/slot_hidden/pallas_call | solution.py:395
  9.4 0.0 collective-permute-done.refs_0_
  9.4 0.3 %collective-permute-start.2 = (bf16[256,256]{1,0:T(8,128)(2,1)S(1)}, bf16[256,256]{1,0:T(8,128)(2,1)S(1)}, u32[]{:S(2)}, u32[]{:S(2)}) collective-permute-start(bf16[256,256]{1,0:T(8,128)(2,1)S(1)} %collective-permute-done.refs_0_), channel_id=1, source_target_pairs={{0,1},{1,0},{2,3},{3,2},{4,5},{5,4},{6,7},{7,6},{8,9},{9,8},{10,11... | collective-permute-start | bytes 393224 | tf_op jit(solution)/shard_map/ppermute | solution.py:341
  9.7 0.0 collective-permute-done.4
  9.7 2.6 %collective-permute-start.5 = (bf16[2,64,152]{2,1,0:T(8,128)(2,1)S(1)}, bf16[2,64,152]{2,1,0:T(8,128)(2,1)S(1)}, u32[]{:S(2)}, u32[]{:S(2)}) collective-permute-start(bf16[2,64,152]{2,1,0:T(8,128)(2,1)S(1)} %pad_maximum_fusion.mine_ref), channel_id=1, source_target_pairs={{0,16},{4,20},{8,24},{12,28},{16,0},{20,4},{24,8},{28,12},{1,17},{... | collective-permute-start | bytes 116744 | tf_op jit(solution)/shard_map/ppermute | solution.py:336
  12.4 0.0 collective-permute-done.1.refs_1_
  12.4 0.0 collective-permute-done.2.refs_2_
  12.4 2.0 %slot_energy.1 = (f32[16,1,128]{2,1,0:T(1,128)}, bf16[1024,256]{1,0:T(8,128)(2,1)S(1)}) custom-call(f32[1,1]{1,0:T(1,128)} %bitcast.2.field_ref, bf16[832,1024]{1,0:T(8,128)(2,1)S(1)} %get-tuple-element.24.hidden_ref, bf16[64,768]{1,0:T(8,128)(2,1)S(1)} %get-tuple-element.25.owner_ref, f32[2,768]{1,0:T(2,128)S(1)} %get-tuple-element.26.elements_ref, ...), custom_call_target="tpu_custom_call" | custom-call | flops 436207616 | bytes 532480 | tf_op jit(solution)/shard_map/slot_energy/pallas_call | solution.py:441
  14.3 4.3 %all-to-all-start = ((f32[16,1,128]{2,1,0:T(1,128)}), f32[16,1,128]{2,1,0:T(1,128)S(1)}, u32[]{:S(2)}, u32[]{:S(2)}) async-start(f32[16,1,128]{2,1,0:T(1,128)} %get-tuple-element.30), calls=%async_computation | async-start | bytes 16384 | tf_op jit(solution)/shard_map/all_to_all | solution.py:346
  18.7 0.0 collective-permute-done.5.moved_ref
  18.7 0.1 pack.1.packed_ref
  18.8 0.6 %collective-permute-start.6 = (bf16[320,128]{1,0:T(8,128)(2,1)S(1)}, bf16[320,128]{1,0:T(8,128)(2,1)S(1)}, u32[]{:S(2)}, u32[]{:S(2)}) collective-permute-start(bf16[320,128]{1,0:T(8,128)(2,1)S(1)} %pack.1.packed_ref), channel_id=1, source_target_pairs={{0,8},{4,12},{8,0},{12,4},{16,24},{20,28},{24,16},{28,20},{1,9},{5... | collective-permute-start | bytes 245768 | tf_op jit(solution)/shard_map/ppermute | solution.py:336
  19.4 0.9 %near_half.1 = (bf16[256,1024]{1,0:T(8,128)(2,1)S(1)}, f32[256,256]{1,0:T(8,128)S(1)}, f32[256,256]{1,0:T(8,128)S(1)}, f32[256,256]{1,0:T(8,128)S(1)}) custom-call(bf16[320,128]{1,0:T(8,128)(2,1)S(1)} %pack.1.packed_ref, bf16[152,1024]{1,0:T(8,128)(2,1)S(1)} %get-tuple-element.33.w1_ref, f32[1,1024]{1,0:T(1,128)S(1)} %get-tuple-element.34.bias_ref, ...), custom_call_target="tpu_custom_call" | custom-call | flops 348127232 | bytes 1310720 | tf_op jit(solution)/shard_map/near_half/pallas_call | solution.py:480
  20.3 3.4 %all-to-all-done.received_ref = f32[16,1,128]{2,1,0:T(1,128)S(1)} async-done(((f32[16,1,128]{2,1,0:T(1,128)}), f32[16,1,128]{2,1,0:T(1,128)S(1)}, u32[]{:S(2)}, u32[]{:S(2)}) %all-to-all-start) | async-done | bytes 8224 | tf_op jit(solution)/shard_map/all_to_all | solution.py:346
  23.7 0.1 collect.1.mine_ref
  23.8 0.1 collective-permute-start.3
  23.8 0.0 collective-permute-done.6.packed_ref
  23.9 1.3 %far_half.1 = (bf16[1536,512]{1,0:T(8,128)(2,1)S(1)}, f32[256,512]{1,0:T(8,128)S(1)}, f32[256,512]{1,0:T(8,128)S(1)}) custom-call(bf16[320,128]{1,0:T(8,128)(2,1)S(1)} %collective-permute-done.6.packed_ref, bf16[152,1024]{1,0:T(8,128)(2,1)S(1)} %get-tuple-element.33.w1_ref, f32[1,1024]{1,0:T(1,128)S(1)} %get-tuple-element.34.bias_ref, ...), custom_call_target="tpu_custom_call" | custom-call | flops 616562688 | bytes 2621440 | tf_op jit(solution)/shard_map/far_half/pallas_call | solution.py:493
  25.1 0.0 collective-permute-done.3.other_ref
  25.1 2.1 %solve.1 = (f32[2,64]{1,0:T(2,128)}, f32[2,64]{1,0:T(2,128)}) custom-call(f32[2,512]{1,0:T(2,128)S(1)} %collect.1.mine_ref, f32[2,512]{1,0:T(2,128)S(1)} %collective-permute-done.3.other_ref, bf16[1536,512]{1,0:T(8,128)(2,1)S(1)} %get-tuple-element.39.overlap_ref, f32[256,512]{1,0:T(8,128)S(1)} %get-tuple-element.40.re_ref, ...), custom_call_target="tpu_custom_call" | custom-call | flops 805306368 | bytes 1024 | tf_op jit(solution)/shard_map/solve/pallas_call | solution.py:501
  (1 shorter events, 0.0 us)
Async XLA Ops:
  0.6 8.8 %collective-permute-start = (bf16[256,256]{1,0:T(8,128)(2,1)}, bf16[256,256]{1,0:T(8,128)(2,1)S(1)}, u32[]{:S(2)}, u32[]{:S(2)}) collective-permute-start(bf16[256,256]{1,0:T(8,128)(2,1)} %own_hbm.1), channel_id=1, source_target_pairs={{0,2},{2,0},{1,3},{3,1},{4,6},{6,4},{5,7},{7,5},{8,10},{10,8},{9,1... | collective-permute-start | bytes 393224 | tf_op jit(solution)/shard_map/ppermute | solution.py:341
  3.6 8.7 %collective-permute-start.1 = (bf16[256,256]{1,0:T(8,128)(2,1)}, bf16[256,256]{1,0:T(8,128)(2,1)S(1)}, u32[]{:S(2)}, u32[]{:S(2)}) collective-permute-start(bf16[256,256]{1,0:T(8,128)(2,1)} %own_hbm.1), channel_id=1, source_target_pairs={{0,1},{1,0},{2,3},{3,2},{4,5},{5,4},{6,7},{7,6},{8,9},{9,8},{10,11... | collective-permute-start | bytes 393224 | tf_op jit(solution)/shard_map/ppermute | solution.py:341
  4.5 5.2 %collective-permute-start.4 = (bf16[1,64,152]{2,1,0:T(8,128)(2,1)S(1)}, bf16[1,64,152]{2,1,0:T(8,128)(2,1)S(1)}, u32[]{:S(2)}, u32[]{:S(2)}) collective-permute-start(bf16[1,64,152]{2,1,0:T(8,128)(2,1)S(1)} %convert_bitcast_fusion), channel_id=1, source_target_pairs={{0,4},{4,0},{8,12},{12,8},{16,20},{20,16},{24,28},{28,24},{1,5},{5... | collective-permute-start | bytes 58376 | tf_op jit(solution)/shard_map/ppermute | solution.py:336
  9.4 3.0 %collective-permute-start.2 = (bf16[256,256]{1,0:T(8,128)(2,1)S(1)}, bf16[256,256]{1,0:T(8,128)(2,1)S(1)}, u32[]{:S(2)}, u32[]{:S(2)}) collective-permute-start(bf16[256,256]{1,0:T(8,128)(2,1)S(1)} %collective-permute-done.refs_0_), channel_id=1, source_target_pairs={{0,1},{1,0},{2,3},{3,2},{4,5},{5,4},{6,7},{7,6},{8,9},{9,8},{10,11... | collective-permute-start | bytes 393224 | tf_op jit(solution)/shard_map/ppermute | solution.py:341
  9.7 9.0 %collective-permute-start.5 = (bf16[2,64,152]{2,1,0:T(8,128)(2,1)S(1)}, bf16[2,64,152]{2,1,0:T(8,128)(2,1)S(1)}, u32[]{:S(2)}, u32[]{:S(2)}) collective-permute-start(bf16[2,64,152]{2,1,0:T(8,128)(2,1)S(1)} %pad_maximum_fusion.mine_ref), channel_id=1, source_target_pairs={{0,16},{4,20},{8,24},{12,28},{16,0},{20,4},{24,8},{28,12},{1,17},{... | collective-permute-start | bytes 116744 | tf_op jit(solution)/shard_map/ppermute | solution.py:336
  14.3 9.3 %all-to-all-start = ((f32[16,1,128]{2,1,0:T(1,128)}), f32[16,1,128]{2,1,0:T(1,128)S(1)}, u32[]{:S(2)}, u32[]{:S(2)}) async-start(f32[16,1,128]{2,1,0:T(1,128)} %get-tuple-element.30), calls=%async_computation | async-start | bytes 16384 | tf_op jit(solution)/shard_map/all_to_all | solution.py:346
  18.8 5.1 %collective-permute-start.6 = (bf16[320,128]{1,0:T(8,128)(2,1)S(1)}, bf16[320,128]{1,0:T(8,128)(2,1)S(1)}, u32[]{:S(2)}, u32[]{:S(2)}) collective-permute-start(bf16[320,128]{1,0:T(8,128)(2,1)S(1)} %pack.1.packed_ref), channel_id=1, source_target_pairs={{0,8},{4,12},{8,0},{12,4},{16,24},{20,28},{24,16},{28,20},{1,9},{5... | collective-permute-start | bytes 245768 | tf_op jit(solution)/shard_map/ppermute | solution.py:336
  23.8 1.4 %collective-permute-start.3 = (f32[2,512]{1,0:T(2,128)S(1)}, f32[2,512]{1,0:T(2,128)S(1)}, u32[]{:S(2)}, u32[]{:S(2)}) collective-permute-start(f32[2,512]{1,0:T(2,128)S(1)} %collect.1.mine_ref), channel_id=1, source_target_pairs={{0,1},{1,0},{2,3},{3,2},{4,5},{5,4},{6,7},{7,6},{8,9},{9,8},{10,11... | collective-permute-start | bytes 12296 | tf_op jit(solution)/shard_map/ppermute | solution.py:336
where the time goes:
time: 27.5 us; the launch traced here: 27.2 us
  starting transfers between devices  12.5 us (45%)
  Pallas kernels  9.04 us (33%)
  waiting for transfers between devices  3.39 us (12%)
  between operations  1.43 us (5%)
  other arithmetic  0.86 us (3%)
    ppermute x4, starting transfers between devices, swap(): lax.ppermute(x, axis, [(i, i ^ bit) for i in range(lax.axis_size(axis))])  4.88 us
    all_to_all x1, starting transfers between devices, exchange_all(): lax.all_to_all(send, ('samples', 'chip'), 0, 0, axis_index_groups=[[(k +...  4.33 us
    all_to_all x1, waiting for transfers between devices, exchange_all(): lax.all_to_all(send, ('samples', 'chip'), 0, 0, axis_index_groups=[[(k +...  3.37 us
    ppermute x3, starting transfers between devices, shift(): return lax.ppermute(x, axis, [(i, (i + step) % size) for i in range(size)])  3.3 us
    pallas_call x1, Pallas kernels, body(): call(functools.partial(slot_hidden_kernel, spread), 8, (jax.ShapeDtypeStr...  2.64 us
    pallas_call x1, Pallas kernels, body(): call(solve_kernel, 5, (jax.ShapeDtypeStruct((2, here), F32),) * 2, name='...  2.09 us
    pallas_call x1, Pallas kernels, body(): call(functools.partial(slot_energy_kernel, tuple(shifts)), 5 + len(shifts...  1.98 us
    pallas_call x1, Pallas kernels, body(): call(far_half_kernel, 9, (jax.ShapeDtypeStruct((3 * total, total), BF16),...  1.26 us
  transfers between devices with their start and end apart: 8, of which 1 were waited for; matrix products, arithmetic and copies ran while one was open for 3% of the time, Pallas kernels for 26%

commit v1 on v0

--- a/solution.py
+++ b/solution.py
@@ -1,4 +1,5 @@
 import functools
+import math
 
 import jax
 import jax.numpy as jnp
@@ -131,33 +132,63 @@
     copies[7].wait()
 
 
+def sine_cosine(x):
+    turns = jnp.floor(x * (2.0 / math.pi) + 0.5)
+    rest = ((x - turns * 1.5703125) - turns * 4.837512969970703125e-4) - turns * 7.549789948768648e-8
+    square = rest * rest
+    sine = (-1.9515295891e-4 * square + 8.3321608736e-3) * square - 1.6666654611e-1
+    sine = rest + rest * square * sine
+    cosine = (2.443315711809948e-5 * square - 1.388731625493765e-3) * square + 4.166664568298827e-2
+    cosine = 1.0 - 0.5 * square + square * square * cosine
+    quarter = turns.astype(jnp.int32) & 3
+    odd = (quarter & 1) == 1
+    high_sine = jnp.where(odd, cosine, sine)
+    high_cosine = jnp.where(odd, sine, cosine)
+    sine = jnp.where(quarter >= 2, -high_sine, high_sine)
+    cosine = jnp.where((quarter == 1) | (quarter == 2), -high_cosine, high_cosine)
+    return sine, cosine
+
+
 def slot_energy_kernel(
     shifts, field_ref, hidden_ref, owner_ref, elements_ref, readout_ref, *refs
 ):
-    shard_refs, (send_ref, second_ref) = refs[: len(shifts)], refs[len(shifts) :]
+    shard_refs, (send_ref, turned_ref, second_scratch) = refs[: len(shifts)], refs[len(shifts) :]
     here, slots = owner_ref.shape
     chips = lax.axis_size("chip")
     chip, core = lax.axis_index("chip"), lax.axis_index("core")
     for (step, other), shard in zip(shifts, shard_refs):
         rows = shard.shape[0]
         source = lax.rem(chip + chips - step, chips) * 2 + (core ^ other)
-        second_ref[pl.ds(pl.multiple_of(source * rows, rows), rows), :] = shard[...]
-    mid = jnp.tanh(dot(second_ref[...], hidden_ref[...], ((0,), (1,))))
+        second_scratch[pl.ds(pl.multiple_of(source * rows, rows), rows), :] = shard[...]
+    turned = second_scratch[...].T
+    turned_ref[...] = turned
     readout = readout_ref[...].T
-    logs_re = jnp.sum(mid * readout[:, 0:1], axis=0, keepdims=True)
-    logs_im = jnp.sum(mid * readout[:, 1:2], axis=0, keepdims=True)
+    readout_re, readout_im = readout[:, 0:1], readout[:, 1:2]
     owner = owner_ref[...]
-    own = jnp.concatenate(parts(logs_re[:, slots:]) + parts(logs_im[:, slots:]), axis=0)
-    parent = dot(own, owner, ((1,), (0,)))
-    diff_re = logs_re[:, :slots] - (parent[0:1] + parent[1:2] + parent[2:3])
-    diff_im = logs_im[:, :slots] - (parent[3:4] + parent[4:5] + parent[5:6])
+    field = field_ref[...]
+
+    def logs(start, stop):
+        mid = jnp.tanh(dot(turned, hidden_ref[start:stop, :], ((1,), (1,))))
+        re = jnp.sum(mid * readout_re, axis=0, keepdims=True)
+        return re, jnp.sum(mid * readout_im, axis=0, keepdims=True)
+
+    own_re, own_im = logs(slots, slots + here)
+    parent = dot(jnp.concatenate(parts(own_re) + parts(own_im), axis=0), owner, ((1,), (0,)))
+    parent_re = parent[0:1] + parent[1:2] + parent[2:3]
+    parent_im = parent[3:4] + parent[4:5] + parent[5:6]
     used = jnp.sum(owner.astype(F32), axis=0, keepdims=True) > 0.0
-    weight = elements_ref[0:1, :] + field_ref[...] * elements_ref[1:2, :]
-    scale = weight * jnp.exp(diff_re)
-    contrib_re = jnp.where(used, scale * jnp.cos(diff_im), 0.0)
-    contrib_im = jnp.where(used, scale * jnp.sin(diff_im), 0.0)
-    contrib = jnp.concatenate(parts(contrib_re) + parts(contrib_im), axis=0)
-    sums = dot(contrib, owner, ((1,), (1,)))
+    weight = elements_ref[0:1, :] + field * elements_ref[1:2, :]
+    sums = jnp.zeros((6, here), F32)
+    for start in range(0, slots, ROWS):
+        stop = min(start + ROWS, slots)
+        log_re, log_im = logs(start, stop)
+        scale = weight[:, start:stop] * jnp.exp(log_re - parent_re[:, start:stop])
+        sine, cosine = sine_cosine(log_im - parent_im[:, start:stop])
+        inside = used[:, start:stop]
+        contrib_re = jnp.where(inside, scale * cosine, 0.0)
+        contrib_im = jnp.where(inside, scale * sine, 0.0)
+        contrib = jnp.concatenate(parts(contrib_re) + parts(contrib_im), axis=0)
+        sums = sums + dot(contrib, owner[:, start:stop], ((1,), (1,)))
     partial_re = sums[0:1] + sums[1:2] + sums[2:3]
     partial_im = sums[3:4] + sums[4:5] + sums[5:6]
     row = jnp.concatenate([partial_re, partial_im], axis=1)
@@ -181,9 +212,9 @@
     )
 
 
-def sample_values(packed_ref, w1_ref, bias_ref, second_ref, readout_ref, size):
+def sample_values(packed_ref, w1_ref, bias_ref, turned_ref, readout_ref, size):
     hidden = jnp.tanh(sample_pre(packed_ref, w1_ref, bias_ref, size)).astype(BF16)
-    mid = jnp.tanh(dot(second_ref[...], hidden, ((0,), (1,))))
+    mid = jnp.tanh(dot(turned_ref[...], hidden, ((1,), (1,))))
     slope = 1.0 - mid * mid
     readout = readout_ref[...].T
     return hidden, slope * readout[:, 0:1], slope * readout[:, 1:2]
@@ -213,9 +244,9 @@
     return pre + dot(tail, w1_ref[full:, :], ((1,), (0,))) + bias_ref[...]
 
 
-def near_half_kernel(packed_ref, w1_ref, bias_ref, second_ref, readout_ref, hidden_ref, overlap_ref, re_ref, im_ref):
+def near_half_kernel(packed_ref, w1_ref, bias_ref, turned_ref, readout_ref, hidden_ref, overlap_ref, re_ref, im_ref):
     size = hidden_ref.shape[0]
-    hidden, re_ref[...], im_ref[...] = sample_values(packed_ref, w1_ref, bias_ref, second_ref, readout_ref, size)
+    hidden, re_ref[...], im_ref[...] = sample_values(packed_ref, w1_ref, bias_ref, turned_ref, readout_ref, size)
     hidden_ref[...] = hidden
     overlap_ref[...] = dot(hidden, hidden, ((1,), (1,)))
 
@@ -224,7 +255,7 @@
     packed_ref,
     w1_ref,
     bias_ref,
-    second_ref,
+    turned_ref,
     readout_ref,
     hidden_ref,
     overlap_ref,
@@ -236,7 +267,7 @@
 ):
     size = hidden_ref.shape[0]
     total = 2 * size
-    hidden, re, im = sample_values(packed_ref, w1_ref, bias_ref, second_ref, readout_ref, size)
+    hidden, re, im = sample_values(packed_ref, w1_ref, bias_ref, turned_ref, readout_ref, size)
     re_ref[:, :size] = near_re_ref[...]
     im_ref[:, :size] = near_im_ref[...]
     re_ref[:, size:] = re
@@ -313,12 +344,12 @@
     change_ref[...] = solve(energy, gram)[:, :width]
 
 
-def wide_solve(energy, occ_stack, first_weight, bias_row, second, readout):
+def wide_solve(energy, occ_stack, first_weight, bias_row, turned, readout):
     here = occ_stack.shape[1]
     occupied = occ_stack.reshape(-1, occ_stack.shape[2])
     pre = dot(occupied, first_weight, ((1,), (0,))) + bias_row
     hidden = jnp.tanh(pre).astype(BF16)
-    mid = jnp.tanh(dot(second, hidden, ((0,), (1,))))
+    mid = jnp.tanh(dot(turned, hidden, ((1,), (1,))))
     slope = 1.0 - mid * mid
     slope_re = slope * readout[0][:, None]
     slope_im = slope * readout[1][:, None]
@@ -438,13 +469,14 @@
     stack = jnp.concatenate([occupied[None], moved], axis=0)
     moved = swap(stack, "samples", bits[1])
 
-    send, second = call(
+    send, turned = call(
         functools.partial(slot_energy_kernel, tuple(shifts)),
         5 + len(shifts),
         (
             jax.ShapeDtypeStruct((blocks * chips, 1, 2 * here), F32),
-            jax.ShapeDtypeStruct((wide, narrow), BF16),
+            jax.ShapeDtypeStruct((narrow, wide), BF16),
         ),
+        [pltpu.VMEM((wide, narrow), BF16)],
         name="slot_energy",
         flops=2 * (slots + here) * wide * narrow,
         transcendentals=(slots + here) * narrow,
@@ -465,17 +497,17 @@
     if total > wide:
         stack = jnp.concatenate([stack, moved], axis=0)
         stack = jnp.concatenate([stack, swap(stack, "samples", bits[-1])], axis=0)
-        return wide_solve(mine + other, stack, first_weight, bias_row, second, readout)
+        return wide_solve(mine + other, stack, first_weight, bias_row, turned, readout)
 
     half = total // 2
-    weights = (w1, bias, second, readout_near)
+    weights = (w1, bias, turned, readout_near)
     full = orbitals // 128 * 128
     packed = call(
         pack_kernel,
         3,
         jax.ShapeDtypeStruct((half + here, full), BF16),
         name="pack",
-    )(stack, moved, second)
+    )(stack, moved, turned)
     far_packed = swap(packed, "samples", bits[-1])
     near = call(
         near_half_kernel,

time: 27.5 us -> 27.8 us (1.011)
  Pallas kernels: 9.04 us -> 9.33 us
    pallas_call x1, Pallas kernels: 1.98 us -> 2.29 us  [body(): call(functools.partial(slot_energy_kernel, tuple(shifts)), 5 + len(shifts...]
where the time goes in v1:
time: 27.8 us; the launch traced here: 27.5 us
  starting transfers between devices  12.5 us (45%)
  Pallas kernels  9.33 us (34%)
  waiting for transfers between devices  3.41 us (12%)
  between operations  1.43 us (5%)
  other arithmetic  0.86 us (3%)
    ppermute x4, starting transfers between devices, swap(): lax.ppermute(x, axis, [(i, i ^ bit) for i in range(lax.axis_size(axis))])  4.88 us
    all_to_all x1, starting transfers between devices, exchange_all(): lax.all_to_all(send, ('samples', 'chip'), 0, 0, axis_index_groups=[[(k +...  4.33 us
    all_to_all x1, waiting for transfers between devices, exchange_all(): lax.all_to_all(send, ('samples', 'chip'), 0, 0, axis_index_groups=[[(k +...  3.39 us
    ppermute x3, starting transfers between devices, shift(): return lax.ppermute(x, axis, [(i, (i + step) % size) for i in range(size)])  3.3 us
    pallas_call x1, Pallas kernels, body(): call(functools.partial(slot_hidden_kernel, spread), 8, (jax.ShapeDtypeStr...  2.64 us
    pallas_call x1, Pallas kernels, body(): call(functools.partial(slot_energy_kernel, tuple(shifts)), 5 + len(shifts...  2.29 us
    pallas_call x1, Pallas kernels, body(): call(solve_kernel, 5, (jax.ShapeDtypeStruct((2, here), F32),) * 2, name='...  2.09 us
    pallas_call x1, Pallas kernels, body(): call(far_half_kernel, 9, (jax.ShapeDtypeStruct((3 * total, total), BF16),...  1.27 us
  transfers between devices with their start and end apart: 8, of which 1 were waited for; matrix products, arithmetic and copies ran while one was open for 3% of the time, Pallas kernels for 26%

profile of v1, /device:TPU:0, one launch (start us, length us, event | category | flops | bytes accessed | tf_op | source)
XLA Modules:
  0.0 27.5 jit_solution(16708988755638246985)
XLA Ops:
  0.6 3.0 %collective-permute-start = (bf16[256,256]{1,0:T(8,128)(2,1)}, bf16[256,256]{1,0:T(8,128)(2,1)S(1)}, u32[]{:S(2)}, u32[]{:S(2)}) collective-permute-start(bf16[256,256]{1,0:T(8,128)(2,1)} %own_hbm.1), channel_id=1, source_target_pairs={{0,2},{2,0},{1,3},{3,1},{4,6},{6,4},{5,7},{7,5},{8,10},{10,8},{9,1... | collective-permute-start | bytes 393224 | tf_op jit(solution)/shard_map/ppermute | solution.py:372
  3.6 0.0 collective-permute-start.1
  3.6 0.8 %convert_bitcast_fusion = bf16[1,64,152]{2,1,0:T(8,128)(2,1)S(1)} fusion(s32[64,152]{1,0:T(8,128)} %occ_hbm.1), kind=kLoop, calls=%fused_computation.1 | loop fusion | flops 9728 | bytes 58368 | tf_op jit(solution)/shard_map/broadcast_in_dim | solution.py:417
  4.5 1.5 %collective-permute-start.4 = (bf16[1,64,152]{2,1,0:T(8,128)(2,1)S(1)}, bf16[1,64,152]{2,1,0:T(8,128)(2,1)S(1)}, u32[]{:S(2)}, u32[]{:S(2)}) collective-permute-start(bf16[1,64,152]{2,1,0:T(8,128)(2,1)S(1)} %convert_bitcast_fusion), channel_id=1, source_target_pairs={{0,4},{4,0},{8,12},{12,8},{16,20},{20,16},{24,28},{28,24},{1,5},{5... | collective-permute-start | bytes 58376 | tf_op jit(solution)/shard_map/ppermute | solution.py:367
  6.0 2.6 %slot_hidden.1 = (bf16[832,1024]{1,0:T(8,128)(2,1)S(1)}, bf16[64,768]{1,0:T(8,128)(2,1)S(1)}, f32[2,768]{1,0:T(2,128)S(1)}, bf16[152,1024]{1,0:T(8,128)(2,1)S(1)...) custom-call(s32[1,64]{1,0:T(1,128)} %bitcast.8, ...), custom_call_target="tpu_custom_call" | custom-call | flops 258998272 | bytes 2276352 | tf_op jit(solution)/shard_map/slot_hidden/pallas_call | solution.py:426
  9.4 0.0 collective-permute-done.refs_0_
  9.4 0.3 %collective-permute-start.2 = (bf16[256,256]{1,0:T(8,128)(2,1)S(1)}, bf16[256,256]{1,0:T(8,128)(2,1)S(1)}, u32[]{:S(2)}, u32[]{:S(2)}) collective-permute-start(bf16[256,256]{1,0:T(8,128)(2,1)S(1)} %collective-permute-done.refs_0_), channel_id=1, source_target_pairs={{0,1},{1,0},{2,3},{3,2},{4,5},{5,4},{6,7},{7,6},{8,9},{9,8},{10,11... | collective-permute-start | bytes 393224 | tf_op jit(solution)/shard_map/ppermute | solution.py:372
  9.7 0.0 collective-permute-done.4
  9.7 2.6 %collective-permute-start.5 = (bf16[2,64,152]{2,1,0:T(8,128)(2,1)S(1)}, bf16[2,64,152]{2,1,0:T(8,128)(2,1)S(1)}, u32[]{:S(2)}, u32[]{:S(2)}) collective-permute-start(bf16[2,64,152]{2,1,0:T(8,128)(2,1)S(1)} %pad_maximum_fusion.mine_ref), channel_id=1, source_target_pairs={{0,16},{4,20},{8,24},{12,28},{16,0},{20,4},{24,8},{28,12},{1,17},{... | collective-permute-start | bytes 116744 | tf_op jit(solution)/shard_map/ppermute | solution.py:367
  12.4 0.0 collective-permute-done.1.refs_1_
  12.4 0.0 collective-permute-done.2.refs_2_
  12.4 2.3 %slot_energy.1 = (f32[16,1,128]{2,1,0:T(1,128)}, bf16[256,1024]{1,0:T(8,128)(2,1)S(1)}) custom-call(f32[1,1]{1,0:T(1,128)} %bitcast.2.field_ref, bf16[832,1024]{1,0:T(8,128)(2,1)S(1)} %get-tuple-element.24.hidden_ref, bf16[64,768]{1,0:T(8,128)(2,1)S(1)} %get-tuple-element.25.owner_ref, f32[2,768]{1,0:T(2,128)S(1)} %get-tuple-element.26.elements_ref, ...), custom_call_target="tpu_custom_call" | custom-call | flops 436207616 | bytes 532480 | tf_op jit(solution)/shard_map/slot_energy/pallas_call | solution.py:472
  14.6 4.3 %all-to-all-start = ((f32[16,1,128]{2,1,0:T(1,128)}), f32[16,1,128]{2,1,0:T(1,128)S(1)}, u32[]{:S(2)}, u32[]{:S(2)}) async-start(f32[16,1,128]{2,1,0:T(1,128)} %get-tuple-element.30), calls=%async_computation | async-start | bytes 16384 | tf_op jit(solution)/shard_map/all_to_all | solution.py:377
  19.0 0.0 collective-permute-done.5.moved_ref
  19.0 0.1 pack.1.packed_ref
  19.1 0.6 %collective-permute-start.6 = (bf16[320,128]{1,0:T(8,128)(2,1)S(1)}, bf16[320,128]{1,0:T(8,128)(2,1)S(1)}, u32[]{:S(2)}, u32[]{:S(2)}) collective-permute-start(bf16[320,128]{1,0:T(8,128)(2,1)S(1)} %pack.1.packed_ref), channel_id=1, source_target_pairs={{0,8},{4,12},{8,0},{12,4},{16,24},{20,28},{24,16},{28,20},{1,9},{5... | collective-permute-start | bytes 245768 | tf_op jit(solution)/shard_map/ppermute | solution.py:367
  19.7 0.9 %near_half.1 = (bf16[256,1024]{1,0:T(8,128)(2,1)S(1)}, f32[256,256]{1,0:T(8,128)S(1)}, f32[256,256]{1,0:T(8,128)S(1)}, f32[256,256]{1,0:T(8,128)S(1)}) custom-call(bf16[320,128]{1,0:T(8,128)(2,1)S(1)} %pack.1.packed_ref, bf16[152,1024]{1,0:T(8,128)(2,1)S(1)} %get-tuple-element.33.w1_ref, f32[1,1024]{1,0:T(1,128)S(1)} %get-tuple-element.34.bias_ref, ...), custom_call_target="tpu_custom_call" | custom-call | flops 348127232 | bytes 1310720 | tf_op jit(solution)/shard_map/near_half/pallas_call | solution.py:512
  20.6 3.4 %all-to-all-done.received_ref = f32[16,1,128]{2,1,0:T(1,128)S(1)} async-done(((f32[16,1,128]{2,1,0:T(1,128)}), f32[16,1,128]{2,1,0:T(1,128)S(1)}, u32[]{:S(2)}, u32[]{:S(2)}) %all-to-all-start) | async-done | bytes 8224 | tf_op jit(solution)/shard_map/all_to_all | solution.py:377
  24.0 0.1 collect.1.mine_ref
  24.1 0.1 collective-permute-start.3
  24.2 0.0 collective-permute-done.6.packed_ref
  24.2 1.3 %far_half.1 = (bf16[1536,512]{1,0:T(8,128)(2,1)S(1)}, f32[256,512]{1,0:T(8,128)S(1)}, f32[256,512]{1,0:T(8,128)S(1)}) custom-call(bf16[320,128]{1,0:T(8,128)(2,1)S(1)} %collective-permute-done.6.packed_ref, bf16[152,1024]{1,0:T(8,128)(2,1)S(1)} %get-tuple-element.33.w1_ref, f32[1,1024]{1,0:T(1,128)S(1)} %get-tuple-element.34.bias_ref, ...), custom_call_target="tpu_custom_call" | custom-call | flops 616562688 | bytes 2621440 | tf_op jit(solution)/shard_map/far_half/pallas_call | solution.py:525
  25.4 0.0 collective-permute-done.3.other_ref
  25.4 2.1 %solve.1 = (f32[2,64]{1,0:T(2,128)}, f32[2,64]{1,0:T(2,128)}) custom-call(f32[2,512]{1,0:T(2,128)S(1)} %collect.1.mine_ref, f32[2,512]{1,0:T(2,128)S(1)} %collective-permute-done.3.other_ref, bf16[1536,512]{1,0:T(8,128)(2,1)S(1)} %get-tuple-element.39.overlap_ref, f32[256,512]{1,0:T(8,128)S(1)} %get-tuple-element.40.re_ref, ...), custom_call_target="tpu_custom_call" | custom-call | flops 805306368 | bytes 1024 | tf_op jit(solution)/shard_map/solve/pallas_call | solution.py:533
  (1 shorter events, 0.0 us)
Async XLA Ops:
  0.6 8.8 %collective-permute-start = (bf16[256,256]{1,0:T(8,128)(2,1)}, bf16[256,256]{1,0:T(8,128)(2,1)S(1)}, u32[]{:S(2)}, u32[]{:S(2)}) collective-permute-start(bf16[256,256]{1,0:T(8,128)(2,1)} %own_hbm.1), channel_id=1, source_target_pairs={{0,2},{2,0},{1,3},{3,1},{4,6},{6,4},{5,7},{7,5},{8,10},{10,8},{9,1... | collective-permute-start | bytes 393224 | tf_op jit(solution)/shard_map/ppermute | solution.py:372
  3.6 8.7 %collective-permute-start.1 = (bf16[256,256]{1,0:T(8,128)(2,1)}, bf16[256,256]{1,0:T(8,128)(2,1)S(1)}, u32[]{:S(2)}, u32[]{:S(2)}) collective-permute-start(bf16[256,256]{1,0:T(8,128)(2,1)} %own_hbm.1), channel_id=1, source_target_pairs={{0,1},{1,0},{2,3},{3,2},{4,5},{5,4},{6,7},{7,6},{8,9},{9,8},{10,11... | collective-permute-start | bytes 393224 | tf_op jit(solution)/shard_map/ppermute | solution.py:372
  4.5 5.2 %collective-permute-start.4 = (bf16[1,64,152]{2,1,0:T(8,128)(2,1)S(1)}, bf16[1,64,152]{2,1,0:T(8,128)(2,1)S(1)}, u32[]{:S(2)}, u32[]{:S(2)}) collective-permute-start(bf16[1,64,152]{2,1,0:T(8,128)(2,1)S(1)} %convert_bitcast_fusion), channel_id=1, source_target_pairs={{0,4},{4,0},{8,12},{12,8},{16,20},{20,16},{24,28},{28,24},{1,5},{5... | collective-permute-start | bytes 58376 | tf_op jit(solution)/shard_map/ppermute | solution.py:367
  9.4 3.0 %collective-permute-start.2 = (bf16[256,256]{1,0:T(8,128)(2,1)S(1)}, bf16[256,256]{1,0:T(8,128)(2,1)S(1)}, u32[]{:S(2)}, u32[]{:S(2)}) collective-permute-start(bf16[256,256]{1,0:T(8,128)(2,1)S(1)} %collective-permute-done.refs_0_), channel_id=1, source_target_pairs={{0,1},{1,0},{2,3},{3,2},{4,5},{5,4},{6,7},{7,6},{8,9},{9,8},{10,11... | collective-permute-start | bytes 393224 | tf_op jit(solution)/shard_map/ppermute | solution.py:372
  9.7 9.3 %collective-permute-start.5 = (bf16[2,64,152]{2,1,0:T(8,128)(2,1)S(1)}, bf16[2,64,152]{2,1,0:T(8,128)(2,1)S(1)}, u32[]{:S(2)}, u32[]{:S(2)}) collective-permute-start(bf16[2,64,152]{2,1,0:T(8,128)(2,1)S(1)} %pad_maximum_fusion.mine_ref), channel_id=1, source_target_pairs={{0,16},{4,20},{8,24},{12,28},{16,0},{20,4},{24,8},{28,12},{1,17},{... | collective-permute-start | bytes 116744 | tf_op jit(solution)/shard_map/ppermute | solution.py:367
  14.6 9.3 %all-to-all-start = ((f32[16,1,128]{2,1,0:T(1,128)}), f32[16,1,128]{2,1,0:T(1,128)S(1)}, u32[]{:S(2)}, u32[]{:S(2)}) async-start(f32[16,1,128]{2,1,0:T(1,128)} %get-tuple-element.30), calls=%async_computation | async-start | bytes 16384 | tf_op jit(solution)/shard_map/all_to_all | solution.py:377
  19.1 5.1 %collective-permute-start.6 = (bf16[320,128]{1,0:T(8,128)(2,1)S(1)}, bf16[320,128]{1,0:T(8,128)(2,1)S(1)}, u32[]{:S(2)}, u32[]{:S(2)}) collective-permute-start(bf16[320,128]{1,0:T(8,128)(2,1)S(1)} %pack.1.packed_ref), channel_id=1, source_target_pairs={{0,8},{4,12},{8,0},{12,4},{16,24},{20,28},{24,16},{28,20},{1,9},{5... | collective-permute-start | bytes 245768 | tf_op jit(solution)/shard_map/ppermute | solution.py:367
  24.1 1.4 %collective-permute-start.3 = (f32[2,512]{1,0:T(2,128)S(1)}, f32[2,512]{1,0:T(2,128)S(1)}, u32[]{:S(2)}, u32[]{:S(2)}) collective-permute-start(f32[2,512]{1,0:T(2,128)S(1)} %collect.1.mine_ref), channel_id=1, source_target_pairs={{0,1},{1,0},{2,3},{3,2},{4,5},{5,4},{6,7},{7,6},{8,9},{9,8},{10,11... | collective-permute-start | bytes 12296 | tf_op jit(solution)/shard_map/ppermute | solution.py:367
